TPU v7x, 32 devices: a whole 2x2x4 slice. The times are simulated.
32 devices in a mesh: docs: 8 (over z, core), protos: 4 (over y, x).
Axes of the slice: x: 2, y: 2, z: 4, core: 2. Of those that a mesh axis runs over, the one named last changes fastest.
Arguments:
- embeddings: bfloat16 [8192, 512], P('docs'), may hold values from -12.5 to 12.5
- prototypes: bfloat16 [65536, 512], P('protos'), may hold values from -4 to 4
Outputs:
- new_prototypes: bfloat16 [65536, 512], P(('protos', 'docs'))
- column_potential: float32 [65536], P('protos')
- row_potential: float32 [8192], P('docs')
All inputs are finite; a program needn't handle non-finite values.
Results may differ from a plain program's by a relative error of at most 0.0035.
Values may be sent and summed in bfloat16 or wider, within the bound.
No kernel may reach another device: no remote copies, remote signals or barrier semaphores. Data moves between devices by JAX's collectives and lax.ppermute only.
A program may use at most 256 MiB of HBM per device.

v0:
```python
import math
import jax
import jax.numpy as jnp
from jax import lax
from jax.sharding import PartitionSpec as P

SWEEPS = 2


def on_device(embeddings, prototypes):
    local_docs = embeddings.shape[0]
    local_protos = prototypes.shape[0]
    total_docs = local_docs * lax.axis_size("docs")
    total_protos = local_protos * lax.axis_size("protos")
    logit_gain = 4.0 / math.sqrt(embeddings.shape[1])
    scores = (
        lax.dot_general(
            embeddings, prototypes, (((1,), (1,)), ((), ())), preferred_element_type=jnp.float32
        )
        * logit_gain
    )
    row_peak = lax.pmax(jnp.max(scores, axis=1), "protos")
    numerators = jnp.exp(scores - row_peak[:, None])
    row_total = lax.psum(jnp.sum(numerators, axis=1), "protos")
    rescale = 1.0
    row_scale = 1.0 / row_total
    row_weight = rescale * row_scale
    col_scale = jnp.zeros((local_protos,), jnp.float32)
    for sweep_index in range(SWEEPS):
        col_local = jnp.dot(
            row_weight,
            numerators,
            precision=lax.Precision.HIGHEST,
            preferred_element_type=jnp.float32,
        )
        col_total = lax.psum(col_local, "docs")
        col_scale = 1.0 / (total_protos * col_total)
        row_local = rescale * jnp.dot(
            numerators,
            col_scale,
            precision=lax.Precision.HIGHEST,
            preferred_element_type=jnp.float32,
        )
        row_sum = lax.psum(row_local, "protos")
        row_scale = 1.0 / (total_docs * row_sum)
        row_weight = rescale * row_scale
    column_potential = jnp.log(total_docs * col_scale)
    row_potential = jnp.log(row_scale * row_total)
    assignment = (numerators * (total_docs * row_weight)[:, None] * col_scale[None, :]).astype(
        jnp.bfloat16
    )
    summed = lax.psum_scatter(
        lax.dot_general(
            assignment, embeddings, (((0,), (0,)), ((), ())), preferred_element_type=jnp.float32
        ),
        "docs",
        scatter_dimension=0,
        tiled=True,
    )
    new_prototypes = (
        summed * lax.rsqrt(jnp.mean(summed * summed, axis=1, keepdims=True) + 1e-06)
    ).astype(jnp.bfloat16)
    return (new_prototypes, column_potential, row_potential)


def solution(mesh):
    placed = (P("docs", None), P("protos", None))
    return jax.shard_map(
        on_device,
        mesh=mesh,
        in_specs=placed,
        out_specs=(P(("protos", "docs"), None), P("protos"), P("docs")),
        check_vma=False,
    )
```

profile of v0, /device:TPU:0, one launch (start us, length us, event | category | flops | bytes accessed | tf_op | source)
XLA Modules:
  0.0 816.3 jit_solution(17064669797004932549)
XLA Ops:
  7.2 0.0 copy-start
  7.2 0.0 all-reduce.3.cloned.1.call-start
  7.2 1.2 copy-done
  8.4 31.5 %multiply_reduce_fusion = (f32[1024]{0:T(1024)S(1)}, f32[1024,16384]{1,0:T(8,128)}) fusion(bf16[1024,512]{1,0:T(8,128)(2,1)S(1)} %copy-done, bf16[16384,512]{1,0:T(8,128)(2,1)} %param.3), kind=kOutput, calls=%fused_computation.2 | convolution fusion | flops 17213423616 | bytes 84938752 | tf_op jit(solution)/shard_map/dot_general | solution.py:17
  39.9 11.3 %pmax.7 = f32[1024]{0:T(1024)S(1)} all-reduce(f32[1024]{0:T(1024)S(1)} %get-tuple-element.7), channel_id=1, replica_groups=mesh['docs'=8,'protos'=4] {'protos'}, use_global_device_ids=true, to_apply=%region_1.0 | all-reduce | flops 1024 | bytes 8192 | tf_op jit(solution)/shard_map/pmax | solution.py:22
  51.2 21.2 %fusion.7 = f32[1024]{0:T(1024)S(1)} fusion(f32[1024]{0:T(1024)S(1)} %pmax.7, f32[1024,16384]{1,0:T(8,128)} %get-tuple-element.8), kind=kLoop, calls=%fused_computation.21 | loop fusion | flops 50330624 | bytes 67117056 | tf_op jit(solution)/shard_map/reduce_sum | solution.py:24
  72.4 8.3 %psum.35 = f32[1024]{0:T(1024)S(1)} all-reduce(f32[1024]{0:T(1024)S(1)} %fusion.7), channel_id=1, replica_groups=mesh['docs'=8,'protos'=4] {'protos'}, use_global_device_ids=true, to_apply=%region_3.0 | all-reduce | flops 1024 | bytes 8192 | tf_op jit(solution)/shard_map/psum | solution.py:24
  80.7 46.4 %fusion.6 = f32[1,16384]{1,0:T(1,128)} fusion(f32[1024,1]{0,1:T(1,128)S(1)} %bitcast.20, f32[1024,16384]{1,0:T(8,128)} %get-tuple-element.8, f32[1024]{0:T(1024)S(1)} %pmax.7), kind=kOutput, calls=%fused_computation.20 | convolution fusion | flops 234881024 | bytes 67182592 | tf_op jit(solution)/shard_map/dot_general | solution.py:30
  127.1 0.0 all-reduce.3.cloned.1.call-update
  127.1 0.6 all-reduce.5.cloned.1.call-start
  127.8 53.4 %all-reduce.3.cloned.1.call-done = f32[16384]{0:T(1024)} async-done(((f32[16384]{0:T(1024)}), f32[16384]{0:T(1024)}) %all-reduce.3.cloned.1.call-update) | async-done | bytes 65552 | tf_op jit(solution)/shard_map/psum | solution.py:36
  181.2 0.9 multiply_divide_fusion.1
  182.1 69.4 %fusion.5 = f32[1,1024]{1,0:T(1,128)S(1)} fusion(f32[16384,1]{0,1:T(1,128)S(1)} %bitcast.16, f32[1024,16384]{1,0:T(8,128)} %get-tuple-element.8, f32[1024]{0:T(1024)S(1)} %pmax.7), kind=kOutput, calls=%fused_computation.19 | convolution fusion | flops 234881024 | bytes 67182592 | tf_op jit(solution)/shard_map/dot_general | solution.py:38
  251.5 10.0 %psum.37 = f32[1024]{0:T(1024)S(1)} all-reduce(f32[1024]{0:T(1024)S(1)} %bitcast.21), channel_id=1, replica_groups=mesh['docs'=8,'protos'=4] {'protos'}, use_global_device_ids=true, to_apply=%region_5.0 | all-reduce | flops 1024 | bytes 8192 | tf_op jit(solution)/shard_map/psum | solution.py:44
  261.5 46.4 %fusion.4 = f32[1,16384]{1,0:T(1,128)} fusion(f32[1024,1]{0,1:T(1,128)S(1)} %bitcast.19, f32[1024,16384]{1,0:T(8,128)} %get-tuple-element.8, f32[1024]{0:T(1024)S(1)} %pmax.7), kind=kOutput, calls=%fused_computation.18 | convolution fusion | flops 234881024 | bytes 67182592 | tf_op jit(solution)/shard_map/dot_general | solution.py:30
  307.9 0.0 all-reduce.5.cloned.1.call-update
  307.9 0.3 reduce-scatter.2.cloned.1.call-start
  308.1 50.7 %all-reduce.5.cloned.1.call-done = f32[16384]{0:T(1024)} async-done(((f32[16384]{0:T(1024)}), f32[16384]{0:T(1024)}) %all-reduce.5.cloned.1.call-update) | async-done | bytes 65552 | tf_op jit(solution)/shard_map/psum | solution.py:36
  358.8 1.5 multiply_log_fusion
  360.3 69.4 %fusion.3 = f32[1,1024]{1,0:T(1,128)S(1)} fusion(f32[16384,1]{0,1:T(1,128)S(1)} %bitcast.15, f32[1024,16384]{1,0:T(8,128)} %get-tuple-element.8, f32[1024]{0:T(1024)S(1)} %pmax.7), kind=kOutput, calls=%fused_computation.17 | convolution fusion | flops 234881024 | bytes 67182592 | tf_op jit(solution)/shard_map/dot_general | solution.py:38
  429.7 10.1 %psum.39 = f32[1024]{0:T(1024)S(1)} all-reduce(f32[1024]{0:T(1024)S(1)} %bitcast.22), channel_id=1, replica_groups=mesh['docs'=8,'protos'=4] {'protos'}, use_global_device_ids=true, to_apply=%region_7.0 | all-reduce | flops 1024 | bytes 8192 | tf_op jit(solution)/shard_map/psum | solution.py:44
  439.8 0.6 multiply_log_fusion.1
  440.4 39.8 %fusion = f32[16384,512]{1,0:T(8,128)} fusion(bf16[1024,512]{1,0:T(8,128)(2,1)S(1)} %copy-done, f32[16384]{0:T(1024)S(1)} %get-tuple-element.4, f32[1024]{0:T(1024)S(1)} %get-tuple-element.6, f32[1024,16384]{1,0:T(8,128)} %get-tuple-element.8, f32[1024]{0:T(1024)S(1)} %pmax.7), kind=kOutput, calls=%fused_computation.3 | convolution fusion | flops 17263755264 | bytes 101785600 | tf_op jit(solution)/shard_map/dot_general | solution.py:53
  480.2 0.0 reduce-scatter.2.cloned.1.call-update
  480.2 322.9 %reduce-scatter.2.cloned.1.call-done = f32[2048,512]{1,0:T(8,128)} async-done(((f32[16384,512]{1,0:T(8,128)}), f32[2048,512]{1,0:T(8,128)}) %reduce-scatter.2.cloned.1.call-update) | async-done | bytes 4194320 | tf_op jit(solution)/shard_map/reduce_scatter | solution.py:52
  803.1 2.5 multiply_reduce_fusion.1
  805.7 3.8 multiply_convert_fusion.2
  (3 shorter events, 0.0 us)
Async XLA Ops:
  7.2 1.2 copy-start
  7.2 174.0 %all-reduce.3.cloned.1.call-start = ((), (), s32[]{:S(2)}) async-start(), calls=%async_computation.1 | async-start | bytes 131072 | tf_op jit(solution)/shard_map/psum | solution.py:36
  127.1 231.7 %all-reduce.5.cloned.1.call-start = ((), (), s32[]{:S(2)}) async-start(), calls=%async_computation.2 | async-start | bytes 131072 | tf_op jit(solution)/shard_map/psum | solution.py:36
  307.9 495.2 %reduce-scatter.2.cloned.1.call-start = ((), (), s32[]{:S(2)}) async-start(), calls=%async_computation.3 | async-start | bytes 37748736 | tf_op jit(solution)/shard_map/reduce_scatter | solution.py:52
Sparse Core Ops, SparseCore 0:
  127.3 53.9 all-reduce.2
  308.0 50.7 all-reduce.4
  480.4 322.6 reduce-scatter.1
where the time goes:
time: 820 us; the launch traced here: 816 us
  waiting for transfers between devices  427 us (52%)
  matrix products  303 us (37%)
  blocking collectives  39.7 us (5%)
  other arithmetic  30.6 us (4%)
  between operations  14.1 us (2%)
    reduce_scatter x1, waiting for transfers between devices, on_device(): lax.psum_scatter(lax.dot_general(assignment, embeddings, (((0,), (0,)), (...  323 us
    dot_general x2, matrix products, on_device(): jnp.dot(numerators, col_scale, precision=lax.Precision.HIGHEST, preferred...  139 us
    psum x2, waiting for transfers between devices, on_device(): col_total = lax.psum(col_local, 'docs')  104 us
    dot_general x2, matrix products, on_device(): jnp.dot(row_weight, numerators, precision=lax.Precision.HIGHEST, preferre...  92.8 us
    dot_general x1, matrix products, on_device(): lax.dot_general(assignment, embeddings, (((0,), (0,)), ((), ())), preferr...  39.8 us
    dot_general x1, matrix products, on_device(): lax.dot_general(embeddings, prototypes, (((1,), (1,)), ((), ())), preferr...  31.5 us
    reduce_sum x1, other arithmetic, on_device(): row_total = lax.psum(jnp.sum(numerators, axis=1), 'protos')  21.2 us
    psum x2, blocking collectives, on_device(): row_sum = lax.psum(row_local, 'protos')  20.1 us
  transfers between devices with their start and end apart: 3, of which 3 were waited for; matrix products, arithmetic and copies ran while one was open for 0% of the time, Pallas kernels for 0%

commit v1 on v0

--- a/solution.py
+++ b/solution.py
@@ -33,7 +33,13 @@
             precision=lax.Precision.HIGHEST,
             preferred_element_type=jnp.float32,
         )
-        col_total = lax.psum(col_local, "docs")
+        size = lax.axis_size("docs")
+        col_total, far = (col_local, 1)
+        while far < size:
+            col_total = col_total + lax.ppermute(
+                col_total, "docs", [(i, i ^ far) for i in range(size)]
+            )
+            far = 2 * far
         col_scale = 1.0 / (total_protos * col_total)
         row_local = rescale * jnp.dot(
             numerators,

time: 820 us -> 737 us (0.90)
  waiting for transfers between devices: 427 us -> 340 us
    psum x2 -> x0, waiting for transfers between devices: 104 us -> none  [on_device(): col_total = lax.psum(col_local, 'docs')]
    ppermute x0 -> x6, waiting for transfers between devices: none -> 13.1 us  [on_device(): lax.ppermute(col_total, 'docs', [(i, i ^ far) for i in range(size)])]
    ppermute x0 -> x6, starting transfers between devices: none -> 8.91 us  [on_device(): lax.ppermute(col_total, 'docs', [(i, i ^ far) for i in range(size)])]
  transfers between devices with their start and end apart: 3 -> 7, of which waited for: 3 -> 7; matrix products, arithmetic and copies ran while one was open for 0% -> 0% of each run, Pallas kernels for 0% -> 0%
where the time goes in v1:
time: 737 us; the launch traced here: 733 us
  waiting for transfers between devices  340 us (46%)
  matrix products  303 us (41%)
  blocking collectives  36.6 us (5%)
  other arithmetic  29 us (4%)
  between operations  14.4 us (2%)
  starting transfers between devices  8.95 us (1%)
    reduce_scatter x1, waiting for transfers between devices, on_device(): lax.psum_scatter(lax.dot_general(assignment, embeddings, (((0,), (0,)), (...  327 us
    dot_general x2, matrix products, on_device(): jnp.dot(numerators, col_scale, precision=lax.Precision.HIGHEST, preferred...  140 us
    dot_general x2, matrix products, on_device(): jnp.dot(row_weight, numerators, precision=lax.Precision.HIGHEST, preferre...  91.7 us
    dot_general x1, matrix products, on_device(): lax.dot_general(assignment, embeddings, (((0,), (0,)), ((), ())), preferr...  40.1 us
    dot_general x1, matrix products, on_device(): lax.dot_general(embeddings, prototypes, (((1,), (1,)), ((), ())), preferr...  31.5 us
    reduce_sum x1, other arithmetic, on_device(): row_total = lax.psum(jnp.sum(numerators, axis=1), 'protos')  21.2 us
    psum x2, blocking collectives, on_device(): row_sum = lax.psum(row_local, 'protos')  17 us
  transfers between devices with their start and end apart: 7, of which 7 were waited for; matrix products, arithmetic and copies ran while one was open for 0% of the time, Pallas kernels for 0%

profile of v1, /device:TPU:0, one launch (start us, length us, event | category | flops | bytes accessed | tf_op | source)
XLA Modules:
  0.0 733.2 jit_solution(2091199620367050467)
XLA Ops:
  7.2 0.0 copy-start
  7.2 0.0 reduce-scatter.2.cloned.1.call-start
  7.2 1.2 copy-done
  8.4 31.5 %multiply_reduce_fusion = (f32[1024]{0:T(1024)S(1)}, f32[1024,16384]{1,0:T(8,128)}) fusion(bf16[1024,512]{1,0:T(8,128)(2,1)S(1)} %copy-done, bf16[16384,512]{1,0:T(8,128)(2,1)} %param.3), kind=kOutput, calls=%fused_computation.2 | convolution fusion | flops 17213423616 | bytes 84938752 | tf_op jit(solution)/shard_map/dot_general | solution.py:17
  39.9 11.3 %pmax.7 = f32[1024]{0:T(1024)S(1)} all-reduce(f32[1024]{0:T(1024)S(1)} %get-tuple-element.7), channel_id=1, replica_groups=mesh['docs'=8,'protos'=4] {'protos'}, use_global_device_ids=true, to_apply=%region_1.0 | all-reduce | flops 1024 | bytes 8192 | tf_op jit(solution)/shard_map/pmax | solution.py:22
  51.2 21.2 %fusion.7 = f32[1024]{0:T(1024)S(1)} fusion(f32[1024]{0:T(1024)S(1)} %pmax.7, f32[1024,16384]{1,0:T(8,128)} %get-tuple-element.8), kind=kLoop, calls=%fused_computation.21 | loop fusion | flops 50330624 | bytes 67117056 | tf_op jit(solution)/shard_map/reduce_sum | solution.py:24
  72.4 8.3 %psum.21 = f32[1024]{0:T(1024)S(1)} all-reduce(f32[1024]{0:T(1024)S(1)} %fusion.7), channel_id=1, replica_groups=mesh['docs'=8,'protos'=4] {'protos'}, use_global_device_ids=true, to_apply=%region_3.0 | all-reduce | flops 1024 | bytes 8192 | tf_op jit(solution)/shard_map/psum | solution.py:24
  80.7 45.8 %fusion.6 = f32[1,16384]{1,0:T(1,128)S(1)} fusion(f32[1024,1]{0,1:T(1,128)S(1)} %bitcast.22, f32[1024,16384]{1,0:T(8,128)} %get-tuple-element.8, f32[1024]{0:T(1024)S(1)} %pmax.7), kind=kOutput, calls=%fused_computation.20 | convolution fusion | flops 234881024 | bytes 67182592 | tf_op jit(solution)/shard_map/dot_general | solution.py:30
  126.5 0.0 collective-permute-start
  126.5 1.3 collective-permute-done
  127.8 1.6 collective-permute-start.1
  129.4 2.7 collective-permute-done.1
  132.1 2.7 collective-permute-start.2
  134.8 2.6 collective-permute-done.2
  137.4 70.0 %fusion.5 = f32[1,1024]{1,0:T(1,128)S(1)} fusion(f32[16384,1]{0,1:T(1,128)S(1)} %bitcast.15, f32[1024,16384]{1,0:T(8,128)} %get-tuple-element.8, f32[1024]{0:T(1024)S(1)} %pmax.7), kind=kOutput, calls=%fused_computation.19 | convolution fusion | flops 234881024 | bytes 67182592 | tf_op jit(solution)/shard_map/dot_general | solution.py:44
  207.3 9.0 %psum.22 = f32[1024]{0:T(1024)S(1)} all-reduce(f32[1024]{0:T(1024)S(1)} %bitcast.23), channel_id=1, replica_groups=mesh['docs'=8,'protos'=4] {'protos'}, use_global_device_ids=true, to_apply=%region_4.0 | all-reduce | flops 1024 | bytes 8192 | tf_op jit(solution)/shard_map/psum | solution.py:50
  216.3 45.9 %fusion.4 = f32[1,16384]{1,0:T(1,128)S(1)} fusion(f32[1024,1]{0,1:T(1,128)S(1)} %bitcast.21, f32[1024,16384]{1,0:T(8,128)} %get-tuple-element.8, f32[1024]{0:T(1024)S(1)} %pmax.7), kind=kOutput, calls=%fused_computation.18 | convolution fusion | flops 234881024 | bytes 67182592 | tf_op jit(solution)/shard_map/dot_general | solution.py:30
  262.2 0.0 collective-permute-start.3
  262.2 1.3 collective-permute-done.3
  263.5 1.6 collective-permute-start.4
  265.2 2.7 collective-permute-done.4
  267.9 3.0 collective-permute-start.5
  270.8 2.6 collective-permute-done.5
  273.4 0.7 multiply_log_fusion
  274.1 69.5 %fusion.3 = f32[1,1024]{1,0:T(1,128)S(1)} fusion(f32[16384,1]{0,1:T(1,128)S(1)} %bitcast.16, f32[1024,16384]{1,0:T(8,128)} %get-tuple-element.8, f32[1024]{0:T(1024)S(1)} %pmax.7), kind=kOutput, calls=%fused_computation.17 | convolution fusion | flops 234881024 | bytes 67182592 | tf_op jit(solution)/shard_map/dot_general | solution.py:44
  343.6 8.0 %psum.23 = f32[1024]{0:T(1024)S(1)} all-reduce(f32[1024]{0:T(1024)S(1)} %bitcast.24), channel_id=1, replica_groups=mesh['docs'=8,'protos'=4] {'protos'}, use_global_device_ids=true, to_apply=%region_5.0 | all-reduce | flops 1024 | bytes 8192 | tf_op jit(solution)/shard_map/psum | solution.py:50
  351.6 0.6 multiply_log_fusion.1
  352.3 40.1 %fusion = f32[16384,512]{1,0:T(8,128)} fusion(bf16[1024,512]{1,0:T(8,128)(2,1)S(1)} %copy-done, f32[16384]{0:T(1024)S(1)} %get-tuple-element.4, f32[1024]{0:T(1024)S(1)} %get-tuple-element.6, f32[1024,16384]{1,0:T(8,128)} %get-tuple-element.8, f32[1024]{0:T(1024)S(1)} %pmax.7), kind=kOutput, calls=%fused_computation.3 | convolution fusion | flops 17263755264 | bytes 101785600 | tf_op jit(solution)/shard_map/dot_general | solution.py:59
  392.3 0.0 reduce-scatter.2.cloned.1.call-update
  392.3 327.3 %reduce-scatter.2.cloned.1.call-done = f32[2048,512]{1,0:T(8,128)} async-done(((f32[16384,512]{1,0:T(8,128)}), f32[2048,512]{1,0:T(8,128)}) %reduce-scatter.2.cloned.1.call-update) | async-done | bytes 4194320 | tf_op jit(solution)/shard_map/reduce_scatter | solution.py:58
  719.7 2.5 multiply_reduce_fusion.1
  722.2 3.8 multiply_convert_fusion.2
  (8 shorter events, 0.1 us)
Async XLA Ops:
  7.2 1.2 copy-start
  7.2 712.5 %reduce-scatter.2.cloned.1.call-start = ((), (), s32[]{:S(2)}) async-start(), calls=%async_computation.1 | async-start | bytes 37748736 | tf_op jit(solution)/shard_map/reduce_scatter | solution.py:58
  126.5 1.3 collective-permute-start
  127.8 4.3 collective-permute-start.1
  132.1 5.2 collective-permute-start.2
  262.2 1.3 collective-permute-start.3
  263.5 4.3 collective-permute-start.4
  267.9 5.6 collective-permute-start.5
Sparse Core Ops, SparseCore 0:
  392.5 327.1 reduce-scatter.1
